TPU v7x, 32 devices: a whole 2x2x4 slice. The times are simulated.
32 devices in a mesh: ctx: 4 (over y, core), ep: 8 (over z, x).
Axes of the slice: x: 2, y: 2, z: 4, core: 2. Of those that a mesh axis runs over, the one named last changes fastest.
Arguments:
- queries: bfloat16 [16, 128, 576], P('ep'), may hold values from -52 to 52
- latent_cache: bfloat16 [16, 1024, 576], P('ep', 'ctx'), may hold values from -6 to 6
- lengths: int32 [16], P('ep'), may hold values from 32 to 1024, as said below
- value_up_weight: bfloat16 [128, 512, 128], P('ctx'), may hold values from -3 to 3
- out_proj: bfloat16 [16384, 7168], P('ctx', 'ep'), may hold values from -0.046875 to 0.046875
- residual: bfloat16 [16, 7168], P('ctx', 'ep'), may hold values from -41 to 41
- norm_gain: bfloat16 [7168], P('ep'), may hold values from 0.5 to 1.5
- expert_ids: int32 [16, 2], replicated, may hold values from 0 to 3, all different within a row; in each aligned block of 16 rows (0 to 15, 16 to 31, ...) at most 12 rows name the same one
- expert_route_weight: float32 [16, 2], replicated, may hold values from 0.1 to 0.5
- gate_proj: bfloat16 [4, 7168, 1024], P('ctx', 'ep'), may hold values from -0.0625 to 0.0625
- up_proj: bfloat16 [4, 7168, 1024], P('ctx', 'ep'), may hold values from -0.0625 to 0.0625
- down_proj: bfloat16 [4, 1024, 7168], P('ctx', None, 'ep'), may hold values from -0.1875 to 0.1875
Outputs:
- layer_out: bfloat16 [16, 7168], P('ctx', 'ep')
Inputs may be any that keep to these rules, and one draw needn't show every extreme that they name: `lengths`: some row has length 1024. `expert_ids`: each row names 2 different experts; no expert is named by more than 12 rows, a bound that some block reaches.
All inputs are finite; a program needn't handle non-finite values.
Results may differ from a plain program's by a relative error of at most 0.0064.
Values may be sent and summed in bfloat16 or wider, within the bound.
A program may use at most 64 MiB of HBM per device.

v0:
```python
import jax
import jax.numpy as jnp
from jax import lax
from jax.sharding import PartitionSpec as P

D = 7168
LATENT = 512
VDIM = 128


SOFTMAX_SCALE = 192.0 ** (-0.5)
EPSILON = 1e-06


def combined_all(array, axis, combine):
    everything = jax.tree.map(lambda part: lax.all_gather(part, axis), array)
    first = jax.tree.map(lambda part: part[0], everything)

    def lap(k, so_far):
        return combine(so_far, jax.tree.map(lambda part: part[k], everything))

    return lax.fori_loop(1, lax.axis_size(axis), lap, first)


def merge_parts(earlier, later):
    left_running_max, total_left, left_numerator = earlier
    peak_right, total_right, numer_right = later
    top_score = jnp.maximum(left_running_max, peak_right)
    factor_left = jnp.exp(left_running_max - top_score)
    factor_right = jnp.exp(peak_right - top_score)
    totals = total_left * factor_left + total_right * factor_right
    numerator = left_numerator * factor_left[..., None] + numer_right * factor_right[..., None]
    return (top_score, totals, numerator)


def local(
    queries,
    latent_cache,
    lengths,
    value_up_weight,
    out_proj,
    residual,
    norm_gain,
    expert_ids,
    expert_route_weight,
    gate_proj,
    up_proj,
    down_proj,
):
    ctx_index = lax.axis_index("ctx")
    expert_count = lax.axis_size("ctx")
    ctx_dev = latent_cache.shape[1]
    head_count = value_up_weight.shape[0]
    all_rows = expert_ids.shape[0]
    top_count = expert_ids.shape[1]
    capacity = all_rows * 3 // 4
    owned_rows = residual.shape[0]
    positions = ctx_index * ctx_dev + lax.iota(jnp.int32, ctx_dev)
    is_valid = (positions[None, :] < lengths[:, None])[:, None, :]
    scores = (
        jnp.einsum("rhk,rpk->rhp", queries, latent_cache, preferred_element_type=jnp.float32)
        * SOFTMAX_SCALE
    )
    masked = jnp.where(is_valid, scores, -1e30)
    top_score = jnp.max(masked, axis=-1)
    weights = jnp.where(is_valid, jnp.exp(masked - top_score[..., None]), 0.0)
    totals = jnp.sum(weights, axis=-1)
    numerator = jnp.einsum(
        "rhp,rpk->rhk",
        weights.astype(jnp.bfloat16),
        latent_cache[:, :, :LATENT],
        preferred_element_type=jnp.float32,
    )
    merged_peak, merged_total, merged_numer = combined_all(
        (top_score, totals, numerator), "ctx", merge_parts
    )
    own_numer = lax.dynamic_slice_in_dim(merged_numer, ctx_index * head_count, head_count, 1)
    own_total = lax.dynamic_slice_in_dim(merged_total, ctx_index * head_count, head_count, 1)
    attention_result = (own_numer / own_total[..., None]).astype(jnp.bfloat16)
    value_per_head = jnp.einsum(
        "dxp,xpz->dxz", attention_result, value_up_weight, preferred_element_type=jnp.float32
    )
    value_per_head = value_per_head.astype(jnp.bfloat16).reshape(
        value_per_head.shape[0], head_count * VDIM
    )
    attn_out = jnp.dot(
        lax.all_gather(value_per_head, "ep", axis=0, tiled=True),
        out_proj,
        preferred_element_type=jnp.float32,
    )
    expert_range = lax.iota(jnp.int32, expert_count)
    chosen = jnp.sum(
        (expert_ids[:, :, None] == expert_range[None, None, :]).astype(jnp.int32), axis=1
    )
    slot_order = jnp.cumsum(chosen, axis=0) - chosen
    slot_range = lax.iota(jnp.int32, capacity)
    slot_table = (
        (chosen.T[:, None, :] == 1) & (slot_order.T[:, None, :] == slot_range[None, :, None])
    ).astype(jnp.float32)
    own_table = lax.dynamic_slice_in_dim(slot_table, ctx_index, 1, 0)[0]
    row_start_own = ctx_index * owned_rows
    own_part = lax.dynamic_slice_in_dim(attn_out, row_start_own, owned_rows, 0) + residual.astype(
        jnp.float32
    )
    attn_with = lax.dynamic_update_slice_in_dim(attn_out, own_part, row_start_own, 0)
    flat_table = slot_table.reshape(expert_count * capacity, all_rows)
    picked = flat_table
    slot_hidden = lax.psum_scatter(
        jnp.dot(picked, attn_with, precision=lax.Precision.HIGHEST),
        "ctx",
        scatter_dimension=0,
        tiled=True,
    ).astype(jnp.bfloat16)
    slot_wide = slot_hidden.astype(jnp.float32)
    square_part = jnp.sum(slot_wide * slot_wide, axis=-1)
    normed = (slot_wide * norm_gain.astype(jnp.float32)).astype(jnp.bfloat16)
    gate_part = jnp.dot(normed, gate_proj[0], preferred_element_type=jnp.float32)
    upper_part = jnp.dot(normed, up_proj[0], preferred_element_type=jnp.float32)
    gate_sum, upper_sum, square_sum = lax.psum((gate_part, upper_part, square_part), "ep")
    inv_rms = lax.rsqrt(square_sum / D + EPSILON)
    expert_hidden = (
        jax.nn.silu(inv_rms[:, None] * gate_sum) * (inv_rms[:, None] * upper_sum)
    ).astype(jnp.bfloat16)
    expert_out = jnp.dot(expert_hidden, down_proj[0], preferred_element_type=jnp.float32)
    own_weight = jnp.sum(jnp.where(expert_ids == ctx_index, expert_route_weight, 0.0), axis=1)
    slot_weight = jnp.dot(own_table, own_weight, precision=lax.Precision.HIGHEST)
    contribution = slot_weight[:, None] * expert_out
    contribution = contribution + slot_wide / top_count
    picked = own_table
    mixed = lax.psum_scatter(
        jnp.einsum("st,sd->td", picked, contribution, precision=lax.Precision.HIGHEST),
        "ctx",
        scatter_dimension=0,
        tiled=True,
    )
    return mixed.astype(jnp.bfloat16)


def solution(mesh):
    placed = (
        P("ep", None, None),
        P("ep", "ctx", None),
        P("ep"),
        P("ctx", None, None),
        P("ctx", "ep"),
        P("ctx", "ep"),
        P("ep"),
        P(),
        P(),
        P("ctx", "ep", None),
        P("ctx", "ep", None),
        P("ctx", None, "ep"),
    )
    return jax.shard_map(
        local, mesh=mesh, in_specs=placed, out_specs=P("ctx", "ep"), check_vma=False
    )
```

profile of v0, /device:TPU:0, one launch (start us, length us, event | category | flops | bytes accessed | tf_op | source)
XLA Modules:
  0.0 187.8 jit_solution(5455922782851656687)
XLA Ops:
  6.6 0.9 broadcast_compare_fusion
  7.4 1.5 fusion.53
  9.0 2.2 %fusion.15 = f32[2,128,512]{2,1,0:T(8,128)} fusion(bf16[2,256,576]{1,2,0:T(8,128)(2,1)} %param.15, f32[2,128,256]{2,1,0:T(8,128)S(1)} %get-tuple-element.210, f32[2,128]{1,0:T(2,128)S(1)} %get-tuple-element.209, pred[2,256]{1,0:T(4,128)(4,1)S(1)} %broadcast_compare_fusion), kind=kOutput, calls=%fused_computation.21 | convolution fusion | flops 67305472 | bytes 1312256 | tf_op jit(solution)/shard_map/rhp,rpk->rhk/dot_general | solution.py:68
  11.7 0.1 eq.66
  11.7 0.2 fusion.18
  11.9 6.0 %all-gather.4 = f32[4,2,128]{2,1,0:T(2,128)S(1)} all-gather(f32[1,2,128]{2,1,0:T(2,128)S(1)} %bitcast.65), channel_id=3, replica_groups=mesh['ctx'=4,'ep'=8] {'ctx'}, dimensions={0}, use_global_device_ids=true | all-gather | bytes 5120 | tf_op jit(solution)/shard_map/all_gather | solution.py:16
  18.0 5.3 %all-gather.3 = f32[4,2,128]{2,1,0:T(2,128)S(1)} all-gather(f32[1,2,128]{2,1,0:T(2,128)S(1)} %bitcast.64), channel_id=2, replica_groups=mesh['ctx'=4,'ep'=8] {'ctx'}, dimensions={0}, use_global_device_ids=true | all-gather | bytes 5120 | tf_op jit(solution)/shard_map/all_gather | solution.py:16
  23.4 13.2 %all-gather.8.cloned.1.call-done = f32[8,128,512]{2,1,0:T(8,128)} async-done(((f32[2,128,512]{2,1,0:T(8,128)}), f32[8,128,512]{2,1,0:T(8,128)}) %all-gather.8.cloned.1.call-update) | async-done | bytes 2097168 | tf_op jit(solution)/shard_map/all_gather | solution.py:16
  36.6 1.1 slice.23
  37.7 3.8 %while.19 = (s32[]{:T(128)}, f32[2,128]{1,0:T(2,128)S(1)}, f32[2,128]{1,0:T(2,128)S(1)}, f32[2,128,512]{2,1,0:T(8,128)S(1)}, f32[4,2,128]{2,1,0:T(2,128)S(1)}, /...) while((s32[]{:T(128)}, f32[2,128]{1,0:T(2,128)S(1)}, ...), condition=%wide.region_6.7_spmd, body=%wide.region_5.6_spmd.sunk | while | flops 394757 | bytes 1583255 | solution.py:22
  37.7 1.2 fusion.64
  39.0 1.2 fusion.64
  40.3 1.2 fusion.64
  41.6 0.1 divide_convert_fusion
  41.7 2.8 %fusion.14 = bf16[1,2,4096]{2,1,0:T(2,128)(2,1)S(1)} fusion(bf16[32,512,128]{2,1,0:T(8,128)(2,1)} %param.17, bf16[2,32,512]{2,1,0:T(8,128)(2,1)S(1)} %divide_convert_fusion), kind=kOutput, calls=%fused_computation.19 | convolution fusion | flops 8396800 | bytes 4276224 | tf_op jit(solution)/shard_map/dxp,xpz->dxz/dot_general | solution.py:80
  44.5 30.6 %all-gather.5 = bf16[8,2,4096]{2,1,0:T(2,128)(2,1)S(1)} all-gather(bf16[1,2,4096]{2,1,0:T(2,128)(2,1)S(1)} %fusion.14), channel_id=1, replica_groups=mesh['ctx'=4,'ep'=8] {'ep'}, dimensions={0}, use_global_device_ids=true | all-gather | bytes 147456 | tf_op jit(solution)/shard_map/all_gather | solution.py:87
  75.2 4.1 %fusion.54 = f32[16,896]{1,0:T(8,128)S(1)} fusion(bf16[16,4096]{1,0:T(8,128)(2,1)S(1)} %reshape.60, bf16[4096,896]{1,0:T(8,128)(2,1)} %param.18), kind=kOutput, calls=%fused_computation.76 | convolution fusion | flops 117440512 | bytes 7528448 | tf_op jit(solution)/shard_map/dot_general | solution.py:86
  79.4 0.3 fusion.38
  79.6 7.8 %fusion = f32[16,896]{1,0:T(8,128)S(1)} fusion(f32[48,896]{1,0:T(8,128)S(1)} %fusion.38), kind=kCustom, calls=%all-reduce-scatter | all-reduce-scatter fusion | flops 57345 | bytes 229888
  87.5 1.3 collective-permute-start
  88.8 0.7 fusion.52
  90.9 0.2 concatenate
  91.1 0.6 fusion.24
  91.7 1.0 fusion.6
  92.7 1.0 fusion.8
  93.7 0.1 convolution_bitcast_fusion
  93.8 72.9 %all-reduce.6.cloned.1.call-done = (f32[12,1024]{1,0:T(8,128)}, f32[12,1024]{1,0:T(8,128)}, f32[12]{0:T(128)}) async-done(((f32[12,1024]{1,0:T(8,128)}, f32[12,1024]{1,0:T(8,128)}, f32[12]{0:T(128)}), (f32[12,1024]{1,0:T(8,128)}, f32[12,1024]{1,0:T(8,128)}, f32[12]{0:T(128)})) %all-reduce.6.cloned.1.call-update) | async-done | bytes 98368 | tf_op jit(solution)/shard_map/psum | solution.py:119
  166.8 0.7 add_rsqrt_fusion
  167.5 2.0 %fusion.11 = f32[12,896]{1,0:T(8,128)S(1)} fusion(bf16[1,1024,896]{2,1,0:T(8,128)(2,1)} %param.25, f32[12,1024]{1,0:T(8,128)} %get-tuple-element.198, f32[12,1024]{1,0:T(8,128)} %get-tuple-element.199, f32[12]{0:T(128)S(1)} %add_rsqrt_fusion, f32[12]{0:T(128)S(1)} %convolution_bitcast_fusion), kind=kOutput, calls=%fused_computation.17 | convolution fusion | flops 22129152 | bytes 1976416 | tf_op jit(solution)/shard_map/dot_general | solution.py:124
  169.4 0.2 fusion.27
  169.7 10.7 %all-reduce.1 = bf16[16,896]{1,0:T(8,128)(2,1)S(1)} all-reduce(f32[16,896]{1,0:T(8,128)S(1)} %fusion.27), channel_id=6, replica_groups=mesh['ctx'=4,'ep'=8] {'ctx'}, use_global_device_ids=true, to_apply=%region_12.13.clone | all-reduce | flops 14336 | bytes 86016
  180.4 0.6 dynamic-slice_convert_fusion.1
  (46 shorter events, 0.8 us)
Async XLA Ops:
  6.5 85.2 %copy-start = (bf16[1,896,1024]{2,1,0:T(8,128)(2,1)S(1)}, bf16[1,896,1024]{2,1,0:T(8,128)(2,1)}, u32[]{:S(2)}) copy-start(bf16[1,896,1024]{2,1,0:T(8,128)(2,1)} %param.24) | copy-start | bytes 5505028
  6.5 4.7 %copy-start.3 = (s32[16,2]{0,1:T(2,128)S(1)}, s32[16,2]{0,1:T(2,128)}, u32[]{:S(2)}) copy-start(s32[16,2]{0,1:T(2,128)} %param.21) | copy-start | bytes 388
  6.5 16.8 %copy-start.6 = (f32[16,2]{0,1:T(2,128)S(1)}, f32[16,2]{0,1:T(2,128)}, u32[]{:S(2)}) copy-start(f32[16,2]{0,1:T(2,128)} %param.22) | copy-start | bytes 388
  6.5 30.1 %all-gather.8.cloned.1.call-start = ((), (), s32[]{:S(2)}) async-start(), calls=%async_computation | async-start | bytes 2621440 | tf_op jit(solution)/shard_map/all_gather | solution.py:16
  11.2 155.6 %all-reduce.6.cloned.1.call-start = ((), (), s32[]{:S(2)}) async-start(), calls=%async_computation.1 | async-start | bytes 263168 | tf_op jit(solution)/shard_map/psum | solution.py:119
  75.1 4.2 %copy-start.2 = (bf16[4,896]{1,0:T(4,128)(2,1)S(1)}, bf16[4,896]{1,0:T(4,128)(2,1)}, u32[]{:S(2)}) copy-start(bf16[4,896]{1,0:T(4,128)(2,1)} %param.19) | copy-start | bytes 21508
  75.2 13.7 %copy-start.4 = (bf16[896]{0:T(1024)(128)(2,1)S(1)}, bf16[896]{0:T(1024)(128)(2,1)}, u32[]{:S(2)}) copy-start(bf16[896]{0:T(1024)(128)(2,1)} %param.20) | copy-start | bytes 5380
  75.2 13.7 %copy-start.5 = (u32[32]{0:T(128)S(1)}, u32[32]{0:T(128)}, u32[]{:S(2)}) copy-start(u32[32]{0:T(128)} %constant.85) | copy-start | bytes 388
  87.5 3.4 %collective-permute-start = (bf16[12,896]{1,0:T(8,128)(2,1)S(1)}, bf16[12,896]{1,0:T(8,128)(2,1)S(1)}, u32[]{:S(2)}, u32[]{:S(2)}) collective-permute-start(bf16[12,896]{1,0:T(8,128)(2,1)S(1)} %slice.24), channel_id=1, source_target_pairs={{0,8},{8,16},{16,24},{1,9},{9,17},{17,25},{2,10},{10,18},{18,26},{... | collective-permute-start | bytes 64520
  91.1 1.6 copy-start.1
Sparse Core Ops, SparseCore 0:
  11.3 25.2 all-gather.7
  93.8 72.9 all-reduce.5
where the time goes:
time: 188 us
  waiting for transfers between devices  86.2 us (46%)
  blocking collectives  60.4 us (32%)
  matrix products  15.3 us (8%)
  between operations  15 us (8%)
  other arithmetic  6.29 us (3%)
  local copies, waits for them, and re-layouts  3.19 us (2%)
    psum x1, waiting for transfers between devices, local(): lax.psum((gate_part, upper_part, square_part), 'ep')  72.9 us
    all_gather x1, blocking collectives, local(): lax.all_gather(value_per_head, 'ep', axis=0, tiled=True)  30.6 us
    unnamed x2, blocking collectives  18.5 us
    all_gather x1, waiting for transfers between devices, combined_all(): everything = jax.tree.map(lambda part: lax.all_gather(part, axis), array)  13.2 us
    all_gather x2, blocking collectives, combined_all(): everything = jax.tree.map(lambda part: lax.all_gather(part, axis), array)  11.4 us
    dot_general x1, matrix products, local(): jnp.dot(lax.all_gather(value_per_head, 'ep', axis=0, tiled=True), out_pro...  4.15 us
  transfers between devices with their start and end apart: 3, of which 2 were waited for; matrix products, arithmetic and copies ran while one was open for 1% of the time, Pallas kernels for 0%

commit v1 on v0

v1 whole, which is shorter than its diff:
```python
import functools

import jax
import jax.numpy as jnp
from jax import lax
from jax.experimental import pallas as pl
from jax.experimental.pallas import tpu as pltpu
from jax.sharding import PartitionSpec as P

LATENT = 512
VDIM = 128
LANES = 128
GROUP = 8
SOFTMAX_SCALE = 192.0 ** (-0.5)
EPSILON = 1e-06
MESH = pl.DeviceIdType.MESH
BF16 = jnp.bfloat16
F32 = jnp.float32


def remote(src, dst, send_sem, recv_sem, axis, peer):
    return pltpu.make_async_remote_copy(
        src_ref=src,
        dst_ref=dst,
        send_sem=send_sem,
        recv_sem=recv_sem,
        device_id={axis: peer},
        device_id_type=MESH,
    )


def total_of(parts):
    result = parts[0]
    for part in parts[1:]:
        result = result + part
    return result


def kernel(
    nc, ne, chunks,
    q_hbm, kv_hbm, len_ref, vup_hbm, wo_hbm, res_ref, gain_ref, ids_ref, rw_ref, wg_hbm, wu_hbm, wd_hbm,
    out_ref,
    q_v, kv_v, vup_v, wo_v, wg_v, wu_v, wd_v,
    num_s, num_r, st_s, st_r, hv_r, ao_r, hid_s, sq_s, sq_r, gu_s, gu_r, eh_r, mo_s, mo_r,
    row_sem, vup_sem, wo_sem, ffn_sem,
    num_ss, num_rs, st_ss, st_rs, hv_ss, hv_rs, ao_ss, ao_rs,
    sq_ss, sq_rs, gu_ss, gu_rs, eh_ss, eh_rs, mo_ss, mo_rs,
):
    c = lax.axis_index("ctx")
    e = lax.axis_index("ep")
    rl, heads, _ = q_v.shape
    positions = kv_v.shape[1]
    hpd = vup_v.shape[0]
    nq = hpd // GROUP
    qw = nq // chunks
    rows = ao_r.shape[1]
    dl = ao_r.shape[2]
    ro = rows // nc
    ffw = wg_v.shape[1]
    blocks = ffw // LANES
    gr = gu_s.shape[1]

    ctx_to = [lax.rem(c + d, nc) for d in range(1, nc)]
    ctx_from = [lax.rem(c + nc - d, nc) for d in range(1, nc)]
    ep_to = [lax.rem(e + d, ne) for d in range(1, ne)]
    ep_from = [lax.rem(e + ne - d, ne) for d in range(1, ne)]

    row_copies = []
    for r in range(rl):
        pair = (
            pltpu.make_async_copy(q_hbm.at[r], q_v.at[r], row_sem.at[r, 0]),
            pltpu.make_async_copy(kv_hbm.at[r], kv_v.at[r], row_sem.at[r, 1]),
        )
        row_copies.append(pair)
        for copy in pair:
            copy.start()

    barrier = pltpu.get_barrier_semaphore()
    for peer in ctx_to:
        pl.semaphore_signal(barrier, inc=1, device_id={"ctx": peer}, device_id_type=MESH)
    for peer in ep_to:
        pl.semaphore_signal(barrier, inc=1, device_id={"ep": peer}, device_id_type=MESH)

    vup_copies, wo_copies = [], []
    for ch in range(chunks):
        some = pl.ds(ch * qw * GROUP, qw * GROUP)
        vup_copies.append(pltpu.make_async_copy(vup_hbm.at[some], vup_v.at[some], vup_sem.at[ch]))
        vup_copies[-1].start()
    for ch in range(chunks):
        some = pl.ds(ch * qw * GROUP * VDIM, qw * GROUP * VDIM)
        wo_copies.append(pltpu.make_async_copy(wo_hbm.at[some], wo_v.at[some], wo_sem.at[ch]))
        wo_copies[-1].start()
    ffn_copies = [
        pltpu.make_async_copy(wg_hbm.at[0], wg_v, ffn_sem.at[0]),
        pltpu.make_async_copy(wu_hbm.at[0], wu_v, ffn_sem.at[1]),
        pltpu.make_async_copy(wd_hbm.at[0], wd_v, ffn_sem.at[2]),
    ]
    for copy in ffn_copies:
        copy.start()

    sends = []

    width = LANES // (2 * rl)
    stat_lane = lax.broadcasted_iota(jnp.int32, (heads, LANES), 1)
    place = c * positions + lax.broadcasted_iota(jnp.int32, (heads, positions), 1)
    stats = jnp.zeros((heads, LANES), F32)
    for r in range(rl):
        for copy in row_copies[r]:
            copy.wait()
        scores = lax.dot_general(
            q_v[r], kv_v[r], (((1,), (1,)), ((), ())), preferred_element_type=F32
        ) * SOFTMAX_SCALE
        valid = place < len_ref[r]
        masked = jnp.where(valid, scores, -1e30)
        top = jnp.max(masked, axis=1, keepdims=True)
        weights = jnp.where(valid, jnp.exp(masked - top), 0.0)
        total = jnp.sum(weights, axis=1, keepdims=True)
        numer = jnp.dot(weights.astype(BF16), kv_v[r, :, :LATENT], preferred_element_type=F32)
        for j in range(nc):
            num_s[j, r] = numer[j * hpd : (j + 1) * hpd].astype(BF16)
        stats = jnp.where(stat_lane >= 2 * r * width, top, stats)
        stats = jnp.where(stat_lane >= (2 * r + 1) * width, total, stats)
        if r == 0:
            pl.semaphore_wait(barrier, nc + ne - 2)
        if r == rl - 1:
            for j in range(nc):
                st_s[j] = stats[j * hpd : (j + 1) * hpd]
            for peer in ctx_to:
                sends.append(remote(st_s.at[peer], st_r.at[c], st_ss.at[peer], st_rs.at[c], "ctx", peer))
                sends[-1].start()
        for peer in ctx_to:
            sends.append(
                remote(num_s.at[peer, r], num_r.at[c, r], num_ss.at[peer, r], num_rs.at[c, r], "ctx", peer)
            )
            sends[-1].start()

    wide = rl * GROUP
    goal = lax.broadcasted_iota(jnp.int32, (rows * GROUP, ne * wide), 0)
    have = lax.broadcasted_iota(jnp.int32, (rows * GROUP, ne * wide), 1)
    target = (
        (have & (GROUP - 1)) * rows
        + lax.shift_right_logical(have, wide.bit_length() - 1) * rl
        + (lax.shift_right_logical(have, GROUP.bit_length() - 1) & (rl - 1))
    )
    shuffle = jnp.where(goal == target, 1.0, 0.0).astype(BF16)

    for src in ctx_from:
        remote(st_s.at[src], st_r.at[src], st_ss.at[src], st_rs.at[src], "ctx", src).wait_recv()
    for r in range(rl):
        for src in ctx_from:
            remote(num_s.at[src, r], num_r.at[src, r], num_ss.at[src, r], num_rs.at[src, r], "ctx", src).wait_recv()
    all_stats = [st_s[c]] + [st_r[src] for src in ctx_from]
    factors = []
    for r in range(rl):
        tops = [s[:, 2 * r * width : 2 * r * width + 1] for s in all_stats]
        totals = [s[:, (2 * r + 1) * width : (2 * r + 1) * width + 1] for s in all_stats]
        best = functools.reduce(jnp.maximum, tops)
        scale = [jnp.exp(t - best) for t in tops]
        whole = 1.0 / total_of([t * s for t, s in zip(totals, scale)])
        factors.append([s * whole for s in scale])
    row_of_group = lax.broadcasted_iota(jnp.int32, (wide, LATENT), 0) & (GROUP - 1)
    for ch in range(chunks):
        first = ch * qw * GROUP
        merged = []
        for r in range(rl):
            some = slice(first, first + qw * GROUP)
            parts = [num_s[c, r, some]] + [num_r[src, r, some] for src in ctx_from]
            merged.append(
                total_of([p.astype(F32) * f[some] for p, f in zip(parts, factors[r])])
            )
        vup_copies[ch].wait()
        values = []
        for q in range(qw):
            left = jnp.concatenate([m[q * GROUP : (q + 1) * GROUP] for m in merged], axis=0)
            left = jnp.concatenate(
                [jnp.where(row_of_group == g, left, 0.0).astype(BF16) for g in range(GROUP)], axis=1
            )
            right = vup_v[first + q * GROUP : first + (q + 1) * GROUP].reshape(GROUP * LATENT, VDIM)
            values.append(jnp.dot(left, right, preferred_element_type=F32).astype(BF16))
        hv_r[ch, e] = jnp.concatenate(values, axis=1) if qw > 1 else values[0]
        for peer in ep_to:
            sends.append(
                remote(hv_r.at[ch, e], hv_r.at[ch, e], hv_ss.at[ch, peer], hv_rs.at[ch, e], "ep", peer)
            )
            sends[-1].start()

    attn = None
    for ch in range(chunks):
        for src in ep_from:
            remote(hv_r.at[ch, src], hv_r.at[ch, src], hv_ss.at[ch, src], hv_rs.at[ch, src], "ep", src).wait_recv()
        came = hv_r[ch].reshape(ne * wide, qw * VDIM)
        sorted_values = jnp.dot(shuffle, came, preferred_element_type=F32).astype(BF16)
        left = jnp.concatenate(
            [
                sorted_values[g * rows : (g + 1) * rows, q * VDIM : (q + 1) * VDIM]
                for q in range(qw)
                for g in range(GROUP)
            ],
            axis=1,
        )
        wo_copies[ch].wait()
        depth = qw * GROUP * VDIM
        part = jnp.dot(left, wo_v[ch * depth : (ch + 1) * depth, :], preferred_element_type=F32)
        attn = part if attn is None else attn + part
    own_rows = lax.broadcasted_iota(jnp.int32, (rows, dl), 0) - c * ro
    spread = jnp.concatenate([res_ref[...].astype(F32)] * nc, axis=0)
    attn = attn + jnp.where((own_rows >= 0) & (own_rows < ro), spread, 0.0)
    ao_r[c] = attn.astype(BF16)
    for peer in ctx_to:
        sends.append(remote(ao_r.at[c], ao_r.at[c], ao_ss.at[peer], ao_rs.at[c], "ctx", peer))
        sends[-1].start()
    for src in ctx_from:
        remote(ao_r.at[src], ao_r.at[src], ao_ss.at[src], ao_rs.at[src], "ctx", src).wait_recv()
        attn = attn + ao_r[src].astype(F32)

    hidden = attn.astype(BF16).astype(F32)
    for j in range(nc):
        hid_s[j] = hidden[j * ro : (j + 1) * ro]
    square = jnp.sum(hidden * hidden, axis=1, keepdims=True)
    high = square.astype(BF16).astype(F32)
    sq_lane = lax.broadcasted_iota(jnp.int32, (rows, LANES), 1)
    both = jnp.where(sq_lane < LANES // 2, high, square - high).astype(BF16)
    for j in range(rows // gr):
        sq_s[j] = both[j * gr : (j + 1) * gr]
    for peer in ep_to:
        sends.append(
            remote(sq_s.at[peer // blocks], sq_r.at[e], sq_ss.at[peer], sq_rs.at[e], "ep", peer)
        )
        sends[-1].start()
    normed = (hidden * gain_ref[...].astype(F32)).astype(BF16)
    ffn_copies[0].wait()
    gate = jnp.dot(normed, wg_v[...], preferred_element_type=F32)
    ffn_copies[1].wait()
    upper = jnp.dot(normed, wu_v[...], preferred_element_type=F32)
    for p in range(ne):
        some = slice(p // blocks * gr, (p // blocks + 1) * gr)
        cols = slice(p % blocks * LANES, (p % blocks + 1) * LANES)
        gu_s[p] = jnp.concatenate([gate[some, cols], upper[some, cols]], axis=1).astype(BF16)
    for peer in ep_to:
        sends.append(remote(gu_s.at[peer], gu_r.at[e], gu_ss.at[peer], gu_rs.at[e], "ep", peer))
        sends[-1].start()
    squares = sq_s[e // blocks].astype(F32)
    sums = gu_s[e].astype(F32)
    for src in ep_from:
        remote(sq_s.at[0], sq_r.at[src], sq_ss.at[src], sq_rs.at[src], "ep", src).wait_recv()
        squares = squares + sq_r[src].astype(F32)
    for src in ep_from:
        remote(gu_s.at[src], gu_r.at[src], gu_ss.at[src], gu_rs.at[src], "ep", src).wait_recv()
        sums = sums + gu_r[src].astype(F32)
    square = squares[:, :1] + squares[:, LANES // 2 : LANES // 2 + 1]
    inv_rms = lax.rsqrt(square / (dl * ne) + EPSILON)
    gate = inv_rms * sums[:, :LANES]
    upper = inv_rms * sums[:, LANES:]
    eh_r[e] = (gate / (1.0 + jnp.exp(-gate)) * upper).astype(BF16)
    for peer in ep_to:
        sends.append(remote(eh_r.at[e], eh_r.at[e], eh_ss.at[peer], eh_rs.at[e], "ep", peer))
        sends[-1].start()
    route = jnp.sum(jnp.where(ids_ref[...] == c, rw_ref[...], 0.0), axis=1, keepdims=True)
    ffn_copies[2].wait()
    for src in ep_from:
        remote(eh_r.at[src], eh_r.at[src], eh_ss.at[src], eh_rs.at[src], "ep", src).wait_recv()

    left = [
        jnp.concatenate([eh_r[j * blocks + b] for b in range(blocks)], axis=1) for j in range(rows // gr)
    ]
    left = jnp.concatenate(left, axis=0) if len(left) > 1 else left[0]
    expert = route * jnp.dot(left, wd_v[...], preferred_element_type=F32)
    for j in range(nc):
        mo_s[j] = expert[j * ro : (j + 1) * ro]
    for peer in ctx_to:
        sends.append(remote(mo_s.at[peer], mo_r.at[c], mo_ss.at[peer], mo_rs.at[c], "ctx", peer))
        sends[-1].start()
    result = hid_s[c] + mo_s[c]
    for src in ctx_from:
        remote(mo_s.at[src], mo_r.at[src], mo_ss.at[src], mo_rs.at[src], "ctx", src).wait_recv()
        result = result + mo_r[src]
    out_ref[...] = result.astype(BF16)
    for copy in sends:
        copy.wait_send()


def local(
    nc, ne, queries, latent_cache, lengths, value_up, out_proj, residual, norm_gain,
    expert_ids, route_weight, gate_proj, up_proj, down_proj,
):
    rl, heads, width = queries.shape
    positions = latent_cache.shape[1]
    hpd = value_up.shape[0]
    ro, dl = residual.shape
    rows = expert_ids.shape[0]
    ffw = gate_proj.shape[2]
    blocks = ffw // LANES
    gr = rows * blocks // ne
    nq = hpd // GROUP
    chunks = 2 if nq % 2 == 0 else 1
    qw = nq // chunks
    wide = rl * GROUP
    vm = pltpu.VMEM
    dma = pltpu.SemaphoreType.DMA
    scratch = [
        vm((rl, heads, width), BF16),
        vm((rl, positions, width), BF16),
        vm(value_up.shape, BF16),
        vm(out_proj.shape, BF16),
        vm(gate_proj.shape[1:], BF16),
        vm(up_proj.shape[1:], BF16),
        vm(down_proj.shape[1:], BF16),
        vm((nc, rl, hpd, LATENT), BF16),
        vm((nc, rl, hpd, LATENT), BF16),
        vm((nc, hpd, LANES), F32),
        vm((nc, hpd, LANES), F32),
        vm((chunks, ne, wide, qw * VDIM), BF16),
        vm((nc, rows, dl), BF16),
        vm((nc, ro, dl), F32),
        vm((rows // gr, gr, LANES), BF16),
        vm((ne, gr, LANES), BF16),
        vm((ne, gr, 2 * LANES), BF16),
        vm((ne, gr, 2 * LANES), BF16),
        vm((ne, gr, LANES), BF16),
        vm((nc, ro, dl), F32),
        vm((nc, ro, dl), F32),
        dma((rl, 2)),
        dma((chunks,)),
        dma((chunks,)),
        dma((3,)),
    ]
    for shape in ((nc, rl), (nc,), (chunks, ne), (nc,), (ne,), (ne,), (ne,), (nc,)):
        scratch += [dma(shape), dma(shape)]
    held = pl.BlockSpec(memory_space=pltpu.VMEM)
    far = pl.BlockSpec(memory_space=pl.ANY)
    weights = value_up.size + out_proj.size + gate_proj.size + up_proj.size + down_proj.size
    return pl.pallas_call(
        functools.partial(kernel, nc, ne, chunks),
        out_shape=jax.ShapeDtypeStruct((ro, dl), BF16),
        in_specs=[
            far, far, pl.BlockSpec(memory_space=pltpu.SMEM), far, far, held, held, held, held, far, far, far,
        ],
        out_specs=held,
        scratch_shapes=scratch,
        compiler_params=pltpu.CompilerParams(
            collective_id=0, has_side_effects=True, vmem_limit_bytes=52 * 2**20
        ),
        cost_estimate=pl.CostEstimate(
            flops=2 * rows * weights, bytes_accessed=2 * weights, transcendentals=rl * heads * positions
        ),
        name="decode_step",
    )(
        queries, latent_cache, lengths, value_up, out_proj, residual, norm_gain.reshape(1, -1),
        expert_ids, route_weight, gate_proj, up_proj, down_proj,
    )


def solution(mesh):
    placed = (
        P("ep", None, None),
        P("ep", "ctx", None),
        P("ep"),
        P("ctx", None, None),
        P("ctx", "ep"),
        P("ctx", "ep"),
        P("ep"),
        P(),
        P(),
        P("ctx", "ep", None),
        P("ctx", "ep", None),
        P("ctx", None, "ep"),
    )
    step = functools.partial(local, mesh.shape["ctx"], mesh.shape["ep"])
    return jax.shard_map(step, mesh=mesh, in_specs=placed, out_specs=P("ctx", "ep"), check_vma=False)
```

time: 188 us -> 40.9 us (0.22)
  waiting for transfers between devices: 86.2 us -> 0 us
  blocking collectives: 60.4 us -> 0 us
  Pallas kernels: 0 us -> 35.3 us
  matrix products: 15.3 us -> 0 us
  between operations: 15 us -> 0.03 us
  other arithmetic: 6.29 us -> 0 us
  local copies, waits for them, and re-layouts: 3.19 us -> 5.34 us
    psum x1 -> x0, waiting for transfers between devices: 72.9 us -> none  [local(): lax.psum((gate_part, upper_part, square_part), 'ep')]
    all_gather x3 -> x0, blocking collectives: 41.9 us -> none  [the longest x1 30.6 us: local(): lax.all_gather(value_per_head, 'ep', axis=0, tiled=True)]
    pallas_call x0 -> x1, Pallas kernels: none -> 35.3 us  [local(): pl.pallas_call(functools.partial(kernel, nc, ne, chunks), out_shape=jax.S...]
    unnamed x2 -> x0, blocking collectives: 18.5 us -> none
    dot_general x10 -> x0, matrix products: 15.3 us -> none  [the longest x1 4.15 us: local(): jnp.dot(lax.all_gather(value_per_head, 'ep', axis=0, tiled=True), out_pro...]
    all_gather x1 -> x0, waiting for transfers between devices: 13.2 us -> none  [combined_all(): everything = jax.tree.map(lambda part: lax.all_gather(part, axis), array)]
    add x7 -> x0, other arithmetic: 3.72 us -> none  [the longest x3 3.63 us: merge_parts(): left_numerator * factor_left[..., None]]
    unnamed x18 -> x9, local copies, waits for them, and re-layouts: 0.96 us -> 4.63 us
  transfers between devices with their start and end apart: 3 -> 0, of which waited for: 2 -> 0; matrix products, arithmetic and copies ran while one was open for 1% -> 0% of each run, Pallas kernels for 0% -> 0%
where the time goes in v1:
time: 40.9 us; the launch traced here: 40.7 us
  Pallas kernels  35.3 us (86%)
  local copies, waits for them, and re-layouts  5.34 us (13%)
    pallas_call x1, Pallas kernels, local(): pl.pallas_call(functools.partial(kernel, nc, ne, chunks), out_shape=jax.S...  35.3 us
    unnamed x9, local copies, waits for them, and re-layouts  4.63 us

profile of v1, /device:TPU:0, one launch (start us, length us, event | category | flops | bytes accessed | tf_op | source)
XLA Modules:
  0.0 40.7 jit_solution(9370142244594013026)
XLA Ops:
  0.0 0.0 copy-start
  0.0 0.0 copy-start.1
  0.0 0.7 %reshape.3.gain_ref = bf16[1,896]{1,0:T(2,128)(2,1)S(1)} reshape(bf16[896]{0:T(1024)(128)(2,1)} %param.18) | data formatting | bytes 3584 | tf_op jit(solution)/shard_map/reshape | solution.py:348
  0.7 0.8 %copy.15.ids_ref = s32[16,2]{1,0:T(8,128)S(1)} copy(s32[16,2]{0,1:T(2,128)} %param.19) | data formatting | bytes 256 | tf_op args[7]
  1.5 0.8 %copy.16.rw_ref = f32[16,2]{1,0:T(8,128)S(1)} copy(f32[16,2]{0,1:T(2,128)} %param.20) | data formatting | bytes 256 | tf_op args[8]
  2.2 1.2 %copy.13.q_hbm = bf16[2,128,576]{2,1,0:T(8,128)(2,1)S(1)} copy(bf16[2,128,576]{1,2,0:T(8,128)(2,1)} %param.12) | data formatting | bytes 589824 | tf_op args[0]
  3.4 1.4 %copy.14.kv_hbm = bf16[2,256,576]{2,1,0:T(8,128)(2,1)S(1)} copy(bf16[2,256,576]{1,2,0:T(8,128)(2,1)} %param.13) | data formatting | bytes 1179648 | tf_op args[1]
  4.8 0.0 copy-done
  4.8 0.0 copy-done.1
  4.8 35.3 %decode_step.1 = bf16[4,896]{1,0:T(4,128)(2,1)S(1)} custom-call(bf16[2,128,576]{2,1,0:T(8,128)(2,1)S(1)} %copy.13.q_hbm, bf16[2,256,576]{2,1,0:T(8,128)(2,1)S(1)} %copy.14.kv_hbm, s32[2]{0:T(128)S(1)} %copy-done.1, bf16[32,512,128]{2,1,0:T(8,128)(2,1)} %vup_hbm.1, bf16[4096,896]{1,0:T(8,128)(2,1)} %wo_hbm.1, bf16[4,896]{1,0:T(4,128)(2,1)S(1)} %copy-done, ...), custom_call_target="tpu_custom_call" | custom-call | flops 272629760 | bytes 17039360 | tf_op jit(solution)/shard_map/decode_step/pallas_call | solution.py:332
  40.1 0.6 %copy.18 = bf16[4,896]{1,0:T(4,128)(2,1)} copy(bf16[4,896]{1,0:T(4,128)(2,1)S(1)} %decode_step.1) | data formatting | bytes 14336
Async XLA Ops:
  0.0 4.8 %copy-start = (bf16[4,896]{1,0:T(4,128)(2,1)S(1)}, bf16[4,896]{1,0:T(4,128)(2,1)}, u32[]{:S(2)}) copy-start(bf16[4,896]{1,0:T(4,128)(2,1)} %res_ref.1) | copy-start | bytes 21508
  0.0 4.8 %copy-start.1 = (s32[2]{0:T(128)S(1)}, s32[2]{0:T(128)}, u32[]{:S(2)}) copy-start(s32[2]{0:T(128)} %len_ref.1) | copy-start | bytes 28

commit v2 on v1

--- a/solution.py
+++ b/solution.py
@@ -29,6 +29,15 @@
     )
 
 
+def flipped(index, bits):
+    result, bit = index, 1
+    while bit <= bits:
+        if bits & bit:
+            result = result + bit - 2 * bit * lax.rem(lax.div(index, bit), 2)
+        bit *= 2
+    return result
+
+
 def total_of(parts):
     result = parts[0]
     for part in parts[1:]:
@@ -38,18 +47,18 @@
 
 def kernel(
     nc, ne, chunks,
-    q_hbm, kv_hbm, len_ref, vup_hbm, wo_hbm, res_ref, gain_ref, ids_ref, rw_ref, wg_hbm, wu_hbm, wd_hbm,
+    q_hbm, kv_hbm, len_hbm, vup_hbm, wo_hbm, res_hbm, gain_hbm, ids_hbm, rw_hbm, wg_hbm, wu_hbm, wd_hbm,
     out_ref,
-    q_v, kv_v, vup_v, wo_v, wg_v, wu_v, wd_v,
+    q_v, kv_v, vup_v, wo_v, wg_v, wu_v, wd_v, len_ref, res_ref, gain_ref, ids_ref, rw_ref,
     num_s, num_r, st_s, st_r, hv_r, ao_r, hid_s, sq_s, sq_r, gu_s, gu_r, eh_r, mo_s, mo_r,
-    row_sem, vup_sem, wo_sem, ffn_sem,
+    row_sem, vup_sem, wo_sem, ffn_sem, small_sem,
     num_ss, num_rs, st_ss, st_rs, hv_ss, hv_rs, ao_ss, ao_rs,
     sq_ss, sq_rs, gu_ss, gu_rs, eh_ss, eh_rs, mo_ss, mo_rs,
 ):
     c = lax.axis_index("ctx")
     e = lax.axis_index("ep")
-    rl, heads, _ = q_v.shape
-    positions = kv_v.shape[1]
+    rl, _, heads = q_v.shape
+    positions = kv_v.shape[2]
     hpd = vup_v.shape[0]
     nq = hpd // GROUP
     qw = nq // chunks
@@ -60,11 +69,16 @@
     blocks = ffw // LANES
     gr = gu_s.shape[1]
 
-    ctx_to = [lax.rem(c + d, nc) for d in range(1, nc)]
-    ctx_from = [lax.rem(c + nc - d, nc) for d in range(1, nc)]
-    ep_to = [lax.rem(e + d, ne) for d in range(1, ne)]
-    ep_from = [lax.rem(e + ne - d, ne) for d in range(1, ne)]
-
+    ctx_peers = [flipped(c, bits) for bits in reversed(range(1, nc))]
+    ep_peers = [flipped(e, bits) for bits in reversed(range(1, ne))]
+
+    small_copies = [
+        pltpu.make_async_copy(src, dst, small_sem.at[k])
+        for k, (src, dst) in enumerate(
+            ((len_hbm, len_ref), (res_hbm, res_ref), (gain_hbm, gain_ref), (ids_hbm, ids_ref), (rw_hbm, rw_ref))
+        )
+    ]
+    small_copies[0].start()
     row_copies = []
     for r in range(rl):
         pair = (
@@ -76,9 +90,9 @@
             copy.start()
 
     barrier = pltpu.get_barrier_semaphore()
-    for peer in ctx_to:
+    for peer in ctx_peers:
         pl.semaphore_signal(barrier, inc=1, device_id={"ctx": peer}, device_id_type=MESH)
-    for peer in ep_to:
+    for peer in ep_peers:
         pl.semaphore_signal(barrier, inc=1, device_id={"ep": peer}, device_id_type=MESH)
 
     vup_copies, wo_copies = [], []
@@ -95,45 +109,40 @@
         pltpu.make_async_copy(wu_hbm.at[0], wu_v, ffn_sem.at[1]),
         pltpu.make_async_copy(wd_hbm.at[0], wd_v, ffn_sem.at[2]),
     ]
-    for copy in ffn_copies:
+    for copy in small_copies[1:] + ffn_copies:
         copy.start()
 
     sends = []
+
+    def settle():
+        for copy in sends:
+            copy.wait_send()
+        sends.clear()
+
 
     width = LANES // (2 * rl)
     stat_lane = lax.broadcasted_iota(jnp.int32, (heads, LANES), 1)
     place = c * positions + lax.broadcasted_iota(jnp.int32, (heads, positions), 1)
     stats = jnp.zeros((heads, LANES), F32)
+    small_copies[0].wait()
     for r in range(rl):
         for copy in row_copies[r]:
             copy.wait()
         scores = lax.dot_general(
-            q_v[r], kv_v[r], (((1,), (1,)), ((), ())), preferred_element_type=F32
+            q_v[r], kv_v[r], (((0,), (0,)), ((), ())), preferred_element_type=F32
         ) * SOFTMAX_SCALE
         valid = place < len_ref[r]
         masked = jnp.where(valid, scores, -1e30)
         top = jnp.max(masked, axis=1, keepdims=True)
         weights = jnp.where(valid, jnp.exp(masked - top), 0.0)
         total = jnp.sum(weights, axis=1, keepdims=True)
-        numer = jnp.dot(weights.astype(BF16), kv_v[r, :, :LATENT], preferred_element_type=F32)
+        numer = lax.dot_general(
+            weights.astype(BF16), kv_v[r, :LATENT], (((1,), (1,)), ((), ())), preferred_element_type=F32
+        )
         for j in range(nc):
             num_s[j, r] = numer[j * hpd : (j + 1) * hpd].astype(BF16)
         stats = jnp.where(stat_lane >= 2 * r * width, top, stats)
         stats = jnp.where(stat_lane >= (2 * r + 1) * width, total, stats)
-        if r == 0:
-            pl.semaphore_wait(barrier, nc + ne - 2)
-        if r == rl - 1:
-            for j in range(nc):
-                st_s[j] = stats[j * hpd : (j + 1) * hpd]
-            for peer in ctx_to:
-                sends.append(remote(st_s.at[peer], st_r.at[c], st_ss.at[peer], st_rs.at[c], "ctx", peer))
-                sends[-1].start()
-        for peer in ctx_to:
-            sends.append(
-                remote(num_s.at[peer, r], num_r.at[c, r], num_ss.at[peer, r], num_rs.at[c, r], "ctx", peer)
-            )
-            sends[-1].start()
-
     wide = rl * GROUP
     goal = lax.broadcasted_iota(jnp.int32, (rows * GROUP, ne * wide), 0)
     have = lax.broadcasted_iota(jnp.int32, (rows * GROUP, ne * wide), 1)
@@ -144,12 +153,24 @@
     )
     shuffle = jnp.where(goal == target, 1.0, 0.0).astype(BF16)
 
-    for src in ctx_from:
+    for j in range(nc):
+        st_s[j] = stats[j * hpd : (j + 1) * hpd]
+    pl.semaphore_wait(barrier, nc + ne - 2)
+    for peer in ctx_peers:
+        sends.append(remote(st_s.at[peer], st_r.at[c], st_ss.at[peer], st_rs.at[c], "ctx", peer))
+        sends[-1].start()
+        for r in range(rl):
+            sends.append(
+                remote(num_s.at[peer, r], num_r.at[c, r], num_ss.at[peer, r], num_rs.at[c, r], "ctx", peer)
+            )
+            sends[-1].start()
+
+    for src in ctx_peers:
         remote(st_s.at[src], st_r.at[src], st_ss.at[src], st_rs.at[src], "ctx", src).wait_recv()
     for r in range(rl):
-        for src in ctx_from:
+        for src in ctx_peers:
             remote(num_s.at[src, r], num_r.at[src, r], num_ss.at[src, r], num_rs.at[src, r], "ctx", src).wait_recv()
-    all_stats = [st_s[c]] + [st_r[src] for src in ctx_from]
+    all_stats = [st_s[c]] + [st_r[src] for src in ctx_peers]
     factors = []
     for r in range(rl):
         tops = [s[:, 2 * r * width : 2 * r * width + 1] for s in all_stats]
@@ -164,7 +185,7 @@
         merged = []
         for r in range(rl):
             some = slice(first, first + qw * GROUP)
-            parts = [num_s[c, r, some]] + [num_r[src, r, some] for src in ctx_from]
+            parts = [num_s[c, r, some]] + [num_r[src, r, some] for src in ctx_peers]
             merged.append(
                 total_of([p.astype(F32) * f[some] for p, f in zip(parts, factors[r])])
             )
@@ -178,15 +199,16 @@
             right = vup_v[first + q * GROUP : first + (q + 1) * GROUP].reshape(GROUP * LATENT, VDIM)
             values.append(jnp.dot(left, right, preferred_element_type=F32).astype(BF16))
         hv_r[ch, e] = jnp.concatenate(values, axis=1) if qw > 1 else values[0]
-        for peer in ep_to:
+        for peer in ep_peers:
             sends.append(
                 remote(hv_r.at[ch, e], hv_r.at[ch, e], hv_ss.at[ch, peer], hv_rs.at[ch, e], "ep", peer)
             )
             sends[-1].start()
 
     attn = None
+    settle()
     for ch in range(chunks):
-        for src in ep_from:
+        for src in ep_peers:
             remote(hv_r.at[ch, src], hv_r.at[ch, src], hv_ss.at[ch, src], hv_rs.at[ch, src], "ep", src).wait_recv()
         came = hv_r[ch].reshape(ne * wide, qw * VDIM)
         sorted_values = jnp.dot(shuffle, came, preferred_element_type=F32).astype(BF16)
@@ -202,14 +224,16 @@
         depth = qw * GROUP * VDIM
         part = jnp.dot(left, wo_v[ch * depth : (ch + 1) * depth, :], preferred_element_type=F32)
         attn = part if attn is None else attn + part
+    small_copies[1].wait()
     own_rows = lax.broadcasted_iota(jnp.int32, (rows, dl), 0) - c * ro
     spread = jnp.concatenate([res_ref[...].astype(F32)] * nc, axis=0)
     attn = attn + jnp.where((own_rows >= 0) & (own_rows < ro), spread, 0.0)
     ao_r[c] = attn.astype(BF16)
-    for peer in ctx_to:
+    for peer in ctx_peers:
         sends.append(remote(ao_r.at[c], ao_r.at[c], ao_ss.at[peer], ao_rs.at[c], "ctx", peer))
         sends[-1].start()
-    for src in ctx_from:
+    settle()
+    for src in ctx_peers:
         remote(ao_r.at[src], ao_r.at[src], ao_ss.at[src], ao_rs.at[src], "ctx", src).wait_recv()
         attn = attn + ao_r[src].astype(F32)
 
@@ -222,29 +246,31 @@
     both = jnp.where(sq_lane < LANES // 2, high, square - high).astype(BF16)
     for j in range(rows // gr):
         sq_s[j] = both[j * gr : (j + 1) * gr]
-    for peer in ep_to:
+    small_copies[2].wait()
+    normed = (hidden * gain_ref[...].astype(F32).reshape(1, dl)).astype(BF16)
+    ffn_copies[0].wait()
+    gate = jnp.dot(normed, wg_v[...], preferred_element_type=F32)
+    for peer in ep_peers:
         sends.append(
             remote(sq_s.at[peer // blocks], sq_r.at[e], sq_ss.at[peer], sq_rs.at[e], "ep", peer)
         )
         sends[-1].start()
-    normed = (hidden * gain_ref[...].astype(F32)).astype(BF16)
-    ffn_copies[0].wait()
-    gate = jnp.dot(normed, wg_v[...], preferred_element_type=F32)
     ffn_copies[1].wait()
     upper = jnp.dot(normed, wu_v[...], preferred_element_type=F32)
     for p in range(ne):
         some = slice(p // blocks * gr, (p // blocks + 1) * gr)
         cols = slice(p % blocks * LANES, (p % blocks + 1) * LANES)
         gu_s[p] = jnp.concatenate([gate[some, cols], upper[some, cols]], axis=1).astype(BF16)
-    for peer in ep_to:
+    for peer in ep_peers:
         sends.append(remote(gu_s.at[peer], gu_r.at[e], gu_ss.at[peer], gu_rs.at[e], "ep", peer))
         sends[-1].start()
+    settle()
     squares = sq_s[e // blocks].astype(F32)
     sums = gu_s[e].astype(F32)
-    for src in ep_from:
+    for src in ep_peers:
         remote(sq_s.at[0], sq_r.at[src], sq_ss.at[src], sq_rs.at[src], "ep", src).wait_recv()
         squares = squares + sq_r[src].astype(F32)
-    for src in ep_from:
+    for src in ep_peers:
         remote(gu_s.at[src], gu_r.at[src], gu_ss.at[src], gu_rs.at[src], "ep", src).wait_recv()
         sums = sums + gu_r[src].astype(F32)
     square = squares[:, :1] + squares[:, LANES // 2 : LANES // 2 + 1]
@@ -252,12 +278,17 @@
     gate = inv_rms * sums[:, :LANES]
     upper = inv_rms * sums[:, LANES:]
     eh_r[e] = (gate / (1.0 + jnp.exp(-gate)) * upper).astype(BF16)
-    for peer in ep_to:
+    for peer in ep_peers:
         sends.append(remote(eh_r.at[e], eh_r.at[e], eh_ss.at[peer], eh_rs.at[e], "ep", peer))
         sends[-1].start()
-    route = jnp.sum(jnp.where(ids_ref[...] == c, rw_ref[...], 0.0), axis=1, keepdims=True)
+    settle()
+    small_copies[3].wait()
+    small_copies[4].wait()
+    route = jnp.sum(jnp.where(ids_ref[...] == c, rw_ref[...], 0.0), axis=0, keepdims=True)
+    diagonal = lax.broadcasted_iota(jnp.int32, (rows, rows), 0) == lax.broadcasted_iota(jnp.int32, (rows, rows), 1)
+    route = jnp.sum(jnp.where(diagonal, route, 0.0), axis=1, keepdims=True)
     ffn_copies[2].wait()
-    for src in ep_from:
+    for src in ep_peers:
         remote(eh_r.at[src], eh_r.at[src], eh_ss.at[src], eh_rs.at[src], "ep", src).wait_recv()
 
     left = [
@@ -267,16 +298,15 @@
     expert = route * jnp.dot(left, wd_v[...], preferred_element_type=F32)
     for j in range(nc):
         mo_s[j] = expert[j * ro : (j + 1) * ro]
-    for peer in ctx_to:
+    for peer in ctx_peers:
         sends.append(remote(mo_s.at[peer], mo_r.at[c], mo_ss.at[peer], mo_rs.at[c], "ctx", peer))
         sends[-1].start()
+    settle()
     result = hid_s[c] + mo_s[c]
-    for src in ctx_from:
+    for src in ctx_peers:
         remote(mo_s.at[src], mo_r.at[src], mo_ss.at[src], mo_rs.at[src], "ctx", src).wait_recv()
         result = result + mo_r[src]
     out_ref[...] = result.astype(BF16)
-    for copy in sends:
-        copy.wait_send()
 
 
 def local(
@@ -298,13 +328,18 @@
     vm = pltpu.VMEM
     dma = pltpu.SemaphoreType.DMA
     scratch = [
-        vm((rl, heads, width), BF16),
-        vm((rl, positions, width), BF16),
+        vm((rl, width, heads), BF16),
+        vm((rl, width, positions), BF16),
         vm(value_up.shape, BF16),
         vm(out_proj.shape, BF16),
         vm(gate_proj.shape[1:], BF16),
         vm(up_proj.shape[1:], BF16),
         vm(down_proj.shape[1:], BF16),
+        pltpu.SMEM((rl,), jnp.int32),
+        vm((ro, dl), BF16),
+        vm((dl,), BF16),
+        vm((expert_ids.shape[1], rows), jnp.int32),
+        vm((expert_ids.shape[1], rows), F32),
         vm((nc, rl, hpd, LATENT), BF16),
         vm((nc, rl, hpd, LATENT), BF16),
         vm((nc, hpd, LANES), F32),
@@ -323,30 +358,27 @@
         dma((chunks,)),
         dma((chunks,)),
         dma((3,)),
+        dma((5,)),
     ]
     for shape in ((nc, rl), (nc,), (chunks, ne), (nc,), (ne,), (ne,), (ne,), (nc,)):
         scratch += [dma(shape), dma(shape)]
-    held = pl.BlockSpec(memory_space=pltpu.VMEM)
-    far = pl.BlockSpec(memory_space=pl.ANY)
     weights = value_up.size + out_proj.size + gate_proj.size + up_proj.size + down_proj.size
     return pl.pallas_call(
         functools.partial(kernel, nc, ne, chunks),
         out_shape=jax.ShapeDtypeStruct((ro, dl), BF16),
-        in_specs=[
-            far, far, pl.BlockSpec(memory_space=pltpu.SMEM), far, far, held, held, held, held, far, far, far,
-        ],
-        out_specs=held,
+        in_specs=[pl.BlockSpec(memory_space=pl.ANY)] * 12,
+        out_specs=pl.BlockSpec(memory_space=pltpu.VMEM),
         scratch_shapes=scratch,
         compiler_params=pltpu.CompilerParams(
-            collective_id=0, has_side_effects=True, vmem_limit_bytes=52 * 2**20
+            collective_id=0, has_side_effects=True, vmem_limit_bytes=63 * 2**20
         ),
         cost_estimate=pl.CostEstimate(
             flops=2 * rows * weights, bytes_accessed=2 * weights, transcendentals=rl * heads * positions
         ),
         name="decode_step",
     )(
-        queries, latent_cache, lengths, value_up, out_proj, residual, norm_gain.reshape(1, -1),
-        expert_ids, route_weight, gate_proj, up_proj, down_proj,
+        queries.transpose(0, 2, 1), latent_cache.transpose(0, 2, 1), lengths, value_up, out_proj, residual,
+        norm_gain, expert_ids.T, route_weight.T, gate_proj, up_proj, down_proj,
     )
 
 

time: 40.9 us -> 36.8 us (0.90)
  local copies, waits for them, and re-layouts: 5.34 us -> 1.29 us
    unnamed x9 -> x1, local copies, waits for them, and re-layouts: 4.63 us -> 1.29 us
    reshape x1 -> x0, local copies, waits for them, and re-layouts: 0.71 us -> none  [local(): norm_gain.reshape(1, -1)]
where the time goes in v2:
time: 36.8 us; the launch traced here: 36.6 us
  Pallas kernels  35.3 us (96%)
  local copies, waits for them, and re-layouts  1.29 us (4%)
    pallas_call x1, Pallas kernels, local(): pl.pallas_call(functools.partial(kernel, nc, ne, chunks), out_shape=jax.S...  35.3 us
    unnamed x1, local copies, waits for them, and re-layouts  1.29 us

profile of v2, /device:TPU:0, one launch (start us, length us, event | category | flops | bytes accessed | tf_op | source)
XLA Modules:
  0.0 36.6 jit_solution(4133573283853852232)
XLA Ops:
  0.0 35.3 %decode_step.1 = bf16[4,896]{1,0:T(4,128)(2,1)} custom-call(bf16[2,576,128]{2,1,0:T(8,128)(2,1)} %bitcast.5, bf16[2,576,256]{2,1,0:T(8,128)(2,1)} %bitcast.4, s32[2]{0:T(128)} %len_hbm.1, bf16[32,512,128]{2,1,0:T(8,128)(2,1)} %vup_hbm.1, bf16[4096,896]{1,0:T(8,128)(2,1)} %wo_hbm.1, bf16[4,896]{1,0:T(4,128)(2,1)} %res_hbm.1, bf16[896]{0:T(1024)(128)(2,1)} %gain_hbm.1, ...), custom_call_target="tpu_custom_call" | custom-call | flops 272629760 | bytes 17039360 | tf_op jit(solution)/shard_map/decode_step/pallas_call | solution.py:366
  35.3 1.3 %copy.14 = bf16[4,896]{1,0:T(4,128)(2,1)} copy(bf16[4,896]{1,0:T(4,128)(2,1)} %decode_step.1) | data formatting | bytes 14336

commit v3 on v2

--- a/solution.py
+++ b/solution.py
@@ -36,6 +36,14 @@
             result = result + bit - 2 * bit * lax.rem(lax.div(index, bit), 2)
         bit *= 2
     return result
+
+
+def bf16_terms(value, count):
+    terms = []
+    for _ in range(count):
+        terms.append(value.astype(BF16).astype(F32))
+        value = value - terms[-1]
+    return terms
 
 
 def total_of(parts):
@@ -60,8 +68,8 @@
     rl, _, heads = q_v.shape
     positions = kv_v.shape[2]
     hpd = vup_v.shape[0]
-    nq = hpd // GROUP
-    qw = nq // chunks
+    hc = hpd // chunks
+    qw = hc // GROUP
     rows = ao_r.shape[1]
     dl = ao_r.shape[2]
     ro = rows // nc
@@ -120,7 +128,8 @@
         sends.clear()
 
 
-    width = LANES // (2 * rl)
+    terms = 5
+    width = LANES // (terms * rl)
     stat_lane = lax.broadcasted_iota(jnp.int32, (heads, LANES), 1)
     place = c * positions + lax.broadcasted_iota(jnp.int32, (heads, positions), 1)
     stats = jnp.zeros((heads, LANES), F32)
@@ -140,9 +149,10 @@
             weights.astype(BF16), kv_v[r, :LATENT], (((1,), (1,)), ((), ())), preferred_element_type=F32
         )
         for j in range(nc):
-            num_s[j, r] = numer[j * hpd : (j + 1) * hpd].astype(BF16)
-        stats = jnp.where(stat_lane >= 2 * r * width, top, stats)
-        stats = jnp.where(stat_lane >= (2 * r + 1) * width, total, stats)
+            for ch in range(chunks):
+                num_s[j, ch, r] = numer[j * hpd + ch * hc : j * hpd + (ch + 1) * hc].astype(BF16)
+        for k, term in enumerate(bf16_terms(top, 3) + bf16_terms(total, 2)):
+            stats = jnp.where(stat_lane >= (terms * r + k) * width, term, stats)
     wide = rl * GROUP
     goal = lax.broadcasted_iota(jnp.int32, (rows * GROUP, ne * wide), 0)
     have = lax.broadcasted_iota(jnp.int32, (rows * GROUP, ne * wide), 1)
@@ -154,38 +164,41 @@
     shuffle = jnp.where(goal == target, 1.0, 0.0).astype(BF16)
 
     for j in range(nc):
-        st_s[j] = stats[j * hpd : (j + 1) * hpd]
+        st_s[j] = stats[j * hpd : (j + 1) * hpd].astype(BF16)
     pl.semaphore_wait(barrier, nc + ne - 2)
     for peer in ctx_peers:
         sends.append(remote(st_s.at[peer], st_r.at[c], st_ss.at[peer], st_rs.at[c], "ctx", peer))
         sends[-1].start()
-        for r in range(rl):
+    for ch in range(chunks):
+        for peer in ctx_peers:
             sends.append(
-                remote(num_s.at[peer, r], num_r.at[c, r], num_ss.at[peer, r], num_rs.at[c, r], "ctx", peer)
+                remote(num_s.at[peer, ch], num_r.at[c, ch], num_ss.at[peer, ch], num_rs.at[c, ch], "ctx", peer)
             )
             sends[-1].start()
 
     for src in ctx_peers:
         remote(st_s.at[src], st_r.at[src], st_ss.at[src], st_rs.at[src], "ctx", src).wait_recv()
-    for r in range(rl):
-        for src in ctx_peers:
-            remote(num_s.at[src, r], num_r.at[src, r], num_ss.at[src, r], num_rs.at[src, r], "ctx", src).wait_recv()
-    all_stats = [st_s[c]] + [st_r[src] for src in ctx_peers]
+    all_stats = [st_s[c].astype(F32)] + [st_r[src].astype(F32) for src in ctx_peers]
     factors = []
     for r in range(rl):
-        tops = [s[:, 2 * r * width : 2 * r * width + 1] for s in all_stats]
-        totals = [s[:, (2 * r + 1) * width : (2 * r + 1) * width + 1] for s in all_stats]
+        lanes = [[s[:, n * width : n * width + 1] for n in range(terms * r, terms * (r + 1))] for s in all_stats]
+        tops = [total_of(t[:3]) for t in lanes]
+        totals = [total_of(t[3:]) for t in lanes]
         best = functools.reduce(jnp.maximum, tops)
         scale = [jnp.exp(t - best) for t in tops]
         whole = 1.0 / total_of([t * s for t, s in zip(totals, scale)])
         factors.append([s * whole for s in scale])
     row_of_group = lax.broadcasted_iota(jnp.int32, (wide, LATENT), 0) & (GROUP - 1)
     for ch in range(chunks):
-        first = ch * qw * GROUP
+        first = ch * hc
+        for src in ctx_peers:
+            remote(
+                num_s.at[src, ch], num_r.at[src, ch], num_ss.at[src, ch], num_rs.at[src, ch], "ctx", src
+            ).wait_recv()
         merged = []
         for r in range(rl):
-            some = slice(first, first + qw * GROUP)
-            parts = [num_s[c, r, some]] + [num_r[src, r, some] for src in ctx_peers]
+            some = slice(first, first + hc)
+            parts = [num_s[c, ch, r]] + [num_r[src, ch, r] for src in ctx_peers]
             merged.append(
                 total_of([p.astype(F32) * f[some] for p, f in zip(parts, factors[r])])
             )
@@ -297,15 +310,15 @@
     left = jnp.concatenate(left, axis=0) if len(left) > 1 else left[0]
     expert = route * jnp.dot(left, wd_v[...], preferred_element_type=F32)
     for j in range(nc):
-        mo_s[j] = expert[j * ro : (j + 1) * ro]
+        mo_s[j] = expert[j * ro : (j + 1) * ro].astype(BF16)
     for peer in ctx_peers:
         sends.append(remote(mo_s.at[peer], mo_r.at[c], mo_ss.at[peer], mo_rs.at[c], "ctx", peer))
         sends[-1].start()
     settle()
-    result = hid_s[c] + mo_s[c]
+    result = hid_s[c] + mo_s[c].astype(F32)
     for src in ctx_peers:
         remote(mo_s.at[src], mo_r.at[src], mo_ss.at[src], mo_rs.at[src], "ctx", src).wait_recv()
-        result = result + mo_r[src]
+        result = result + mo_r[src].astype(F32)
     out_ref[...] = result.astype(BF16)
 
 
@@ -340,10 +353,10 @@
         vm((dl,), BF16),
         vm((expert_ids.shape[1], rows), jnp.int32),
         vm((expert_ids.shape[1], rows), F32),
-        vm((nc, rl, hpd, LATENT), BF16),
-        vm((nc, rl, hpd, LATENT), BF16),
-        vm((nc, hpd, LANES), F32),
-        vm((nc, hpd, LANES), F32),
+        vm((nc, chunks, rl, hpd // chunks, LATENT), BF16),
+        vm((nc, chunks, rl, hpd // chunks, LATENT), BF16),
+        vm((nc, hpd, LANES), BF16),
+        vm((nc, hpd, LANES), BF16),
         vm((chunks, ne, wide, qw * VDIM), BF16),
         vm((nc, rows, dl), BF16),
         vm((nc, ro, dl), F32),
@@ -352,15 +365,15 @@
         vm((ne, gr, 2 * LANES), BF16),
         vm((ne, gr, 2 * LANES), BF16),
         vm((ne, gr, LANES), BF16),
-        vm((nc, ro, dl), F32),
-        vm((nc, ro, dl), F32),
+        vm((nc, ro, dl), BF16),
+        vm((nc, ro, dl), BF16),
         dma((rl, 2)),
         dma((chunks,)),
         dma((chunks,)),
         dma((3,)),
         dma((5,)),
     ]
-    for shape in ((nc, rl), (nc,), (chunks, ne), (nc,), (ne,), (ne,), (ne,), (nc,)):
+    for shape in ((nc, chunks), (nc,), (chunks, ne), (nc,), (ne,), (ne,), (ne,), (nc,)):
         scratch += [dma(shape), dma(shape)]
     weights = value_up.size + out_proj.size + gate_proj.size + up_proj.size + down_proj.size
     return pl.pallas_call(

time: 36.8 us -> 35.6 us (0.967)
  Pallas kernels: 35.3 us -> 34.1 us
    pallas_call x1, Pallas kernels: 35.3 us -> 34.1 us  [local(): pl.pallas_call(functools.partial(kernel, nc, ne, chunks), out_shape=jax.S...]
where the time goes in v3:
time: 35.6 us; the launch traced here: 35.4 us
  Pallas kernels  34.1 us (96%)
  local copies, waits for them, and re-layouts  1.29 us (4%)
    pallas_call x1, Pallas kernels, local(): pl.pallas_call(functools.partial(kernel, nc, ne, chunks), out_shape=jax.S...  34.1 us
    unnamed x1, local copies, waits for them, and re-layouts  1.29 us

profile of v3, /device:TPU:0, one launch (start us, length us, event | category | flops | bytes accessed | tf_op | source)
XLA Modules:
  0.0 35.4 jit_solution(12491192737490773643)
XLA Ops:
  0.0 34.1 %decode_step.1 = bf16[4,896]{1,0:T(4,128)(2,1)} custom-call(bf16[2,576,128]{2,1,0:T(8,128)(2,1)} %bitcast.5, bf16[2,576,256]{2,1,0:T(8,128)(2,1)} %bitcast.4, s32[2]{0:T(128)} %len_hbm.1, bf16[32,512,128]{2,1,0:T(8,128)(2,1)} %vup_hbm.1, bf16[4096,896]{1,0:T(8,128)(2,1)} %wo_hbm.1, bf16[4,896]{1,0:T(4,128)(2,1)} %res_hbm.1, bf16[896]{0:T(1024)(128)(2,1)} %gain_hbm.1, ...), custom_call_target="tpu_custom_call" | custom-call | flops 272629760 | bytes 17039360 | tf_op jit(solution)/shard_map/decode_step/pallas_call | solution.py:379
  34.1 1.3 %copy.14 = bf16[4,896]{1,0:T(4,128)(2,1)} copy(bf16[4,896]{1,0:T(4,128)(2,1)} %decode_step.1) | data formatting | bytes 14336

commit v4 on v3

--- a/solution.py
+++ b/solution.py
@@ -58,7 +58,7 @@
     q_hbm, kv_hbm, len_hbm, vup_hbm, wo_hbm, res_hbm, gain_hbm, ids_hbm, rw_hbm, wg_hbm, wu_hbm, wd_hbm,
     out_ref,
     q_v, kv_v, vup_v, wo_v, wg_v, wu_v, wd_v, len_ref, res_ref, gain_ref, ids_ref, rw_ref,
-    num_s, num_r, st_s, st_r, hv_r, ao_r, hid_s, sq_s, sq_r, gu_s, gu_r, eh_r, mo_s, mo_r,
+    num_s, num_r, st_s, st_r, hv_r, ao_a, ao_b, hid_s, sq_s, sq_r, gu_s, gu_r, eh_r, mo_s, mo_r,
     row_sem, vup_sem, wo_sem, ffn_sem, small_sem,
     num_ss, num_rs, st_ss, st_rs, hv_ss, hv_rs, ao_ss, ao_rs,
     sq_ss, sq_rs, gu_ss, gu_rs, eh_ss, eh_rs, mo_ss, mo_rs,
@@ -70,8 +70,11 @@
     hpd = vup_v.shape[0]
     hc = hpd // chunks
     qw = hc // GROUP
-    rows = ao_r.shape[1]
-    dl = ao_r.shape[2]
+    rows = ids_ref.shape[1]
+    dl = wo_v.shape[1]
+    ao_r = (ao_a, ao_b)
+    cut = ao_a.shape[2]
+    cuts = (slice(0, cut), slice(cut, dl))
     ro = rows // nc
     ffw = wg_v.shape[1]
     blocks = ffw // LANES
@@ -218,37 +221,52 @@
             )
             sends[-1].start()
 
-    attn = None
     settle()
+    lefts = []
     for ch in range(chunks):
         for src in ep_peers:
             remote(hv_r.at[ch, src], hv_r.at[ch, src], hv_ss.at[ch, src], hv_rs.at[ch, src], "ep", src).wait_recv()
         came = hv_r[ch].reshape(ne * wide, qw * VDIM)
         sorted_values = jnp.dot(shuffle, came, preferred_element_type=F32).astype(BF16)
-        left = jnp.concatenate(
-            [
-                sorted_values[g * rows : (g + 1) * rows, q * VDIM : (q + 1) * VDIM]
-                for q in range(qw)
-                for g in range(GROUP)
-            ],
-            axis=1,
+        lefts.append(
+            jnp.concatenate(
+                [
+                    sorted_values[g * rows : (g + 1) * rows, q * VDIM : (q + 1) * VDIM]
+                    for q in range(qw)
+                    for g in range(GROUP)
+                ],
+                axis=1,
+            )
         )
         wo_copies[ch].wait()
-        depth = qw * GROUP * VDIM
-        part = jnp.dot(left, wo_v[ch * depth : (ch + 1) * depth, :], preferred_element_type=F32)
-        attn = part if attn is None else attn + part
     small_copies[1].wait()
+    depth = hc * VDIM
     own_rows = lax.broadcasted_iota(jnp.int32, (rows, dl), 0) - c * ro
     spread = jnp.concatenate([res_ref[...].astype(F32)] * nc, axis=0)
-    attn = attn + jnp.where((own_rows >= 0) & (own_rows < ro), spread, 0.0)
-    ao_r[c] = attn.astype(BF16)
-    for peer in ctx_peers:
-        sends.append(remote(ao_r.at[c], ao_r.at[c], ao_ss.at[peer], ao_rs.at[c], "ctx", peer))
-        sends[-1].start()
+    spread = jnp.where((own_rows >= 0) & (own_rows < ro), spread, 0.0)
+    parts = []
+    for k, cols in enumerate(cuts):
+        parts.append(
+            spread[:, cols]
+            + total_of(
+                [
+                    jnp.dot(left, wo_v[ch * depth : (ch + 1) * depth, cols], preferred_element_type=F32)
+                    for ch, left in enumerate(lefts)
+                ]
+            )
+        )
+        ao_r[k][c] = parts[-1].astype(BF16)
+        for peer in ctx_peers:
+            sends.append(
+                remote(ao_r[k].at[c], ao_r[k].at[c], ao_ss.at[k, peer], ao_rs.at[k, c], "ctx", peer)
+            )
+            sends[-1].start()
     settle()
-    for src in ctx_peers:
-        remote(ao_r.at[src], ao_r.at[src], ao_ss.at[src], ao_rs.at[src], "ctx", src).wait_recv()
-        attn = attn + ao_r[src].astype(F32)
+    for k in range(len(cuts)):
+        for src in ctx_peers:
+            remote(ao_r[k].at[src], ao_r[k].at[src], ao_ss.at[k, src], ao_rs.at[k, src], "ctx", src).wait_recv()
+            parts[k] = parts[k] + ao_r[k][src].astype(F32)
+    attn = jnp.concatenate(parts, axis=1) if len(parts) > 1 else parts[0]
 
     hidden = attn.astype(BF16).astype(F32)
     for j in range(nc):
@@ -338,6 +356,7 @@
     chunks = 2 if nq % 2 == 0 else 1
     qw = nq // chunks
     wide = rl * GROUP
+    cut = pl.cdiv(dl, 2 * LANES) * LANES
     vm = pltpu.VMEM
     dma = pltpu.SemaphoreType.DMA
     scratch = [
@@ -358,7 +377,8 @@
         vm((nc, hpd, LANES), BF16),
         vm((nc, hpd, LANES), BF16),
         vm((chunks, ne, wide, qw * VDIM), BF16),
-        vm((nc, rows, dl), BF16),
+        vm((nc, rows, cut), BF16),
+        vm((nc, rows, dl - cut), BF16),
         vm((nc, ro, dl), F32),
         vm((rows // gr, gr, LANES), BF16),
         vm((ne, gr, LANES), BF16),
@@ -373,7 +393,7 @@
         dma((3,)),
         dma((5,)),
     ]
-    for shape in ((nc, chunks), (nc,), (chunks, ne), (nc,), (ne,), (ne,), (ne,), (nc,)):
+    for shape in ((nc, chunks), (nc,), (chunks, ne), (2, nc), (ne,), (ne,), (ne,), (nc,)):
         scratch += [dma(shape), dma(shape)]
     weights = value_up.size + out_proj.size + gate_proj.size + up_proj.size + down_proj.size
     return pl.pallas_call(

time: 35.6 us -> 35.4 us (level)
  no operation moved by 1% of the time
where the time goes in v4:
time: 35.4 us; the launch traced here: 35.2 us
  Pallas kernels  33.9 us (96%)
  local copies, waits for them, and re-layouts  1.29 us (4%)
    pallas_call x1, Pallas kernels, local(): pl.pallas_call(functools.partial(kernel, nc, ne, chunks), out_shape=jax.S...  33.9 us
    unnamed x1, local copies, waits for them, and re-layouts  1.29 us

profile of v4, /device:TPU:0, one launch (start us, length us, event | category | flops | bytes accessed | tf_op | source)
XLA Modules:
  0.0 35.2 jit_solution(6256137904762091520)
XLA Ops:
  0.0 33.9 %decode_step.1 = bf16[4,896]{1,0:T(4,128)(2,1)} custom-call(bf16[2,576,128]{2,1,0:T(8,128)(2,1)} %bitcast.5, bf16[2,576,256]{2,1,0:T(8,128)(2,1)} %bitcast.4, s32[2]{0:T(128)} %len_hbm.1, bf16[32,512,128]{2,1,0:T(8,128)(2,1)} %vup_hbm.1, bf16[4096,896]{1,0:T(8,128)(2,1)} %wo_hbm.1, bf16[4,896]{1,0:T(4,128)(2,1)} %res_hbm.1, bf16[896]{0:T(1024)(128)(2,1)} %gain_hbm.1, ...), custom_call_target="tpu_custom_call" | custom-call | flops 272629760 | bytes 17039360 | tf_op jit(solution)/shard_map/decode_step/pallas_call | solution.py:399
  33.9 1.3 %copy.14 = bf16[4,896]{1,0:T(4,128)(2,1)} copy(bf16[4,896]{1,0:T(4,128)(2,1)} %decode_step.1) | data formatting | bytes 14336
